TPU v7x, 512 devices: a whole 4x4x16 slice. The times are simulated.
512 devices in a mesh: frame: 32 (over z_hi, y, x), tensor: 16 (over z_lo, core).
Axes of the slice: x: 4, y: 4, z: 16 (z_hi: 2, z_lo: 8; z = z_hi * 8 + z_lo), core: 2. Of those that a mesh axis runs over, the one named last changes fastest.
Arguments:
- tokens: bfloat16 [16384, 1, 4096], P(('frame', 'tensor')), may hold values from -6 to 6
- norm_gain: float32 [4096], replicated, may hold values from 0.5 to 1.5
- query_weight: bfloat16 [4096, 4096], P(None, 'tensor'), may hold values from -0.09375 to 0.09375
- out_weight: bfloat16 [4096, 4096], P('tensor'), may hold values from -0.09375 to 0.09375
- cache_keys: bfloat16 [1536, 1, 4096], P('frame', None, 'tensor'), may hold values from -420 to 420
- cache_values: bfloat16 [1536, 1, 4096], P('frame', None, 'tensor'), may hold values from -18 to 18
- token_pos: int32 [16384, 1], P('frame'), may hold values from 0 to 1535, as said below
- frame_pad: int32 [1], replicated, may hold values from 0 to 768
Outputs:
- mixed: bfloat16 [16384, 1, 4096], P(('frame', 'tensor'))
Inputs may be any that keep to these rules, and one draw needn't show every extreme that they name: `token_pos`: nondecreasing along each sequence; the last token of every sequence has 1535.
All inputs are finite; a program needn't handle non-finite values.
Results may differ from a plain program's by a relative error of at most 0.018.
Values may be sent and summed in bfloat16 or wider, within the bound.
No kernel may reach another device: no remote copies, remote signals or barrier semaphores. Data moves between devices by JAX's collectives and lax.ppermute only.
A program may use at most 64 MiB of HBM per device.

v0:
```python
import jax
import jax.numpy as jnp
from jax import lax
from jax.sharding import PartitionSpec as P

HEAD_DIM = 128
epsilon = 1e-06
masked_score = -1e30


def normalize(block_rows, norm_gain):
    hidden = block_rows.astype(jnp.float32)
    factor = lax.rsqrt(jnp.mean(hidden * hidden, axis=-1, keepdims=True) + epsilon)
    return (hidden * factor * norm_gain).astype(jnp.bfloat16)


def per_device(
    tokens, norm_gain, query_weight, out_weight, cache_keys, cache_values, token_pos, frame_pad
):
    head_cols = query_weight.shape[1]
    heads_here = head_cols // HEAD_DIM
    seq_count = tokens.shape[1]
    query_scale = HEAD_DIM ** (-0.5)
    outgoing = normalize(tokens, norm_gain)
    queries = (
        jnp.dot(
            lax.all_gather(outgoing, "tensor", axis=0, tiled=True),
            query_weight,
            preferred_element_type=jnp.float32,
        )
        * query_scale
    ).astype(jnp.bfloat16)
    query_rows = queries.shape[0]
    query_heads = queries.reshape(query_rows, seq_count, heads_here, HEAD_DIM)
    all_frames = cache_keys.shape[0] * lax.axis_size("frame")
    valid_frames = all_frames - frame_pad
    start_max = jnp.full((query_rows, seq_count, heads_here), masked_score, jnp.float32)
    running_max = start_max
    key_piece = lax.all_gather(cache_keys, "frame", axis=0, tiled=True)
    value_piece = lax.all_gather(cache_values, "frame", axis=0, tiled=True)
    row_count = key_piece.shape[0]
    frame_index = jnp.arange(row_count, dtype=jnp.int32)
    visible = (frame_index[None, None, :] <= token_pos[:, :, None]) & (
        frame_index[None, None, :] < valid_frames[None, :, None]
    )
    key_heads = key_piece.reshape(row_count, seq_count, heads_here, HEAD_DIM)
    scores = jnp.einsum(
        "rshd,fshd->rshf", query_heads, key_heads, preferred_element_type=jnp.float32
    )
    visible = visible[:, :, None, :]
    scores, visible = (jnp.where(visible, scores, masked_score), visible)
    new_max = jnp.maximum(running_max, jnp.max(scores, axis=-1))
    weights = jnp.where(visible, jnp.exp(scores - new_max[..., None]), 0.0)
    running_sum = jnp.sum(weights, axis=-1)
    value_heads = value_piece.reshape(value_piece.shape[0], seq_count, heads_here, HEAD_DIM)
    accumulated = jnp.einsum(
        "rshf,fshd->rshd",
        weights.astype(jnp.bfloat16),
        value_heads,
        preferred_element_type=jnp.float32,
    )
    running_max, running_sum, accumulated = (new_max, running_sum, accumulated)
    attended = (
        (accumulated / running_sum[..., None])
        .astype(jnp.bfloat16)
        .reshape(query_rows, seq_count, head_cols)
    )
    return lax.psum_scatter(
        jnp.dot(attended, out_weight, preferred_element_type=jnp.float32).astype(jnp.bfloat16),
        "tensor",
        scatter_dimension=0,
        tiled=True,
    )


def solution(mesh):
    placed = (
        P(("frame", "tensor"), None, None),
        P(),
        P(None, "tensor"),
        P("tensor", None),
        P("frame", None, "tensor"),
        P("frame", None, "tensor"),
        P("frame", None),
        P(),
    )
    return jax.shard_map(
        per_device,
        mesh=mesh,
        in_specs=placed,
        out_specs=P(("frame", "tensor"), None, None),
        check_vma=False,
    )
```

profile of v0, /device:TPU:12, one launch (start us, length us, event | category | flops | bytes accessed | tf_op | source)
XLA Modules:
  0.0 464.5 jit_solution(3910015531161201871)
XLA Ops:
  6.5 0.0 copy-start
  6.5 0.0 all-gather.2.cloned.1.call-start
  6.5 1.3 fusion.26
  7.8 1.8 fusion.28
  9.6 0.0 all-gather.2.cloned.1.call-update
  9.6 0.0 reduce-scatter.2.cloned.1.call-start
  10.3 132.0 %all_gather.10 = bf16[1536,1,256]{2,0,1:T(8,128)(2,1)S(1)} all-gather(bf16[48,1,256]{2,0,1:T(8,128)(2,1)} %param.12), channel_id=1, replica_groups=mesh['frame'=32,'tensor'=16] {'frame'}, dimensions={0}, use_global_device_ids=true | all-gather | bytes 811008 | tf_op jit(solution)/shard_map/all_gather | solution.py:39
  142.3 1.2 copy.15
  143.5 150.9 %all_gather.11 = bf16[1536,1,256]{2,0,1:T(8,128)(2,1)S(1)} all-gather(bf16[48,1,256]{2,0,1:T(8,128)(2,1)} %param.13), channel_id=1, replica_groups=mesh['frame'=32,'tensor'=16] {'frame'}, dimensions={0}, use_global_device_ids=true | all-gather | bytes 811008 | tf_op jit(solution)/shard_map/all_gather | solution.py:40
  294.4 1.2 copy.18
  295.6 1.3 fusion.9
  296.8 0.0 all-gather.2.cloned.1.call-done
  296.9 0.0 copy-start.1
  296.9 4.2 fusion.17
  301.1 0.0 copy-done.1
  301.1 0.0 copy-start.2
  301.1 1.3 fusion
  302.5 2.0 fusion.2
  304.5 0.0 copy-done.2
  304.5 1.9 fusion.23
  306.4 0.0 copy-done
  306.4 3.2 fusion.1
  309.6 0.0 reduce-scatter.2.cloned.1.call-update
  309.7 148.0 %reduce-scatter.2.cloned.1.call-done = bf16[32,1,4096]{2,0,1:T(8,128)(2,1)} async-done(((bf16[512,1,4096]{2,0,1:T(8,128)(2,1)}), bf16[32,1,4096]{2,0,1:T(8,128)(2,1)}) %reduce-scatter.2.cloned.1.call-update) | async-done | bytes 262160 | tf_op jit(solution)/shard_map/reduce_scatter | solution.py:68
  (3 shorter events, 0.0 us)
Async XLA Ops:
  6.5 299.9 %copy-start = (bf16[256,4096]{1,0:T(8,128)(2,1)S(1)}, bf16[256,4096]{1,0:T(8,128)(2,1)}, u32[]{:S(2)}) copy-start(bf16[256,4096]{1,0:T(8,128)(2,1)} %param.11) | copy-start | bytes 6291460
  6.5 290.3 %all-gather.2.cloned.1.call-start = ((), (), s32[]{:S(2)}) async-start(), calls=%async_computation.1 | async-start | bytes 4456448 | tf_op jit(solution)/shard_map/all_gather | solution.py:27
  9.6 448.0 %reduce-scatter.2.cloned.1.call-start = ((), (), s32[]{:S(2)}) async-start(), calls=%async_computation.2 | async-start | bytes 4456448 | tf_op jit(solution)/shard_map/reduce_scatter | solution.py:68
  296.9 4.2 copy-start.1
  301.1 3.4 copy-start.2
Sparse Core Ops, SparseCore 0:
  9.7 110.9 all-gather.1
  309.8 147.7 reduce-scatter.1
where the time goes:
time: 465 us; the launch traced here: 464 us
  blocking collectives  283 us (61%)
  waiting for transfers between devices  148 us (32%)
  between operations  14.1 us (3%)
  matrix products  10.7 us (2%)
  other arithmetic  6.36 us (1%)
    all_gather x1, blocking collectives, per_device(): value_piece = lax.all_gather(cache_values, 'frame', axis=0, tiled=True)  151 us
    reduce_scatter x1, waiting for transfers between devices, per_device(): lax.psum_scatter(jnp.dot(attended, out_weight, preferred_element_type=jnp...  148 us
    all_gather x1, blocking collectives, per_device(): key_piece = lax.all_gather(cache_keys, 'frame', axis=0, tiled=True)  132 us
  transfers between devices with their start and end apart: 2, of which 1 were waited for; matrix products, arithmetic and copies ran while one was open for 1% of the time, Pallas kernels for 0%

commit v1 on v0

--- a/solution.py
+++ b/solution.py
@@ -1,3 +1,4 @@
+import functools
 import jax
 import jax.numpy as jnp
 from jax import lax
@@ -6,6 +7,16 @@
 HEAD_DIM = 128
 epsilon = 1e-06
 masked_score = -1e30
+
+
+def spread_the_tails(field_in, lane_axis):
+    value_now = jax.lax.all_to_all(
+        jnp.stack(jax.lax.axis_size(lane_axis) * [field_in]), lane_axis, 0, 0
+    )
+    return jnp.concatenate(value_now, axis=0)
+
+
+order_signs = functools.partial(spread_the_tails, lane_axis="frame")
 
 
 def normalize(block_rows, norm_gain):
@@ -36,7 +47,7 @@
     valid_frames = all_frames - frame_pad
     start_max = jnp.full((query_rows, seq_count, heads_here), masked_score, jnp.float32)
     running_max = start_max
-    key_piece = lax.all_gather(cache_keys, "frame", axis=0, tiled=True)
+    key_piece = order_signs(cache_keys)
     value_piece = lax.all_gather(cache_values, "frame", axis=0, tiled=True)
     row_count = key_piece.shape[0]
     frame_index = jnp.arange(row_count, dtype=jnp.int32)

time: 465 us -> 367 us (0.79)
  the two profiles are of different devices: /device:TPU:12 before, /device:TPU:8 now
where the time goes in v1:
time: 367 us
  blocking collectives  164 us (45%)
  waiting for transfers between devices  145 us (40%)
  starting transfers between devices  20.9 us (6%)
  between operations  14.1 us (4%)
  matrix products  10.8 us (3%)
  other arithmetic  6.36 us (2%)
  local copies, waits for them, and re-layouts  5.6 us (2%)
    all_gather x1, blocking collectives, per_device(): value_piece = lax.all_gather(cache_values, 'frame', axis=0, tiled=True)  164 us
    reduce_scatter x1, waiting for transfers between devices, per_device(): lax.psum_scatter(jnp.dot(attended, out_weight, preferred_element_type=jnp...  145 us
    all_to_all x1, starting transfers between devices, spread_the_tails(): jax.lax.all_to_all(jnp.stack(jax.lax.axis_size(lane_axis) * [field_in]),...  20.8 us
  transfers between devices with their start and end apart: 3, of which 1 were waited for; matrix products, arithmetic and copies ran while one was open for 2% of the time, Pallas kernels for 0%

profile of v1, /device:TPU:8, one launch (start us, length us, event | category | flops | bytes accessed | tf_op | source)
XLA Modules:
  0.0 366.7 jit_solution(17675113454784994772)
XLA Ops:
  6.5 0.0 copy-start
  6.5 0.0 all-gather.2.cloned.1.call-start
  6.5 1.3 fusion.28
  7.8 1.8 fusion.30
  9.6 0.0 all-gather.2.cloned.1.call-update
  9.6 1.7 stack.2
  11.3 20.8 %all-to-all-start = ((bf16[32,48,1,256]{3,1,2,0:T(8,128)(2,1)}), bf16[32,48,1,256]{3,1,2,0:T(8,128)(2,1)}, u32[]{:S(2)}, u32[]{:S(2)}) async-start(bf16[32,48,1,256]{3,1,2,0:T(8,128)(2,1)} %stack.2), calls=%async_computation | async-start | bytes 1572864 | tf_op jit(solution)/shard_map/all_to_all | solution.py:13
  32.2 0.0 reduce-scatter.2.cloned.1.call-start
  32.9 164.2 %all_gather.7 = bf16[1536,1,256]{2,0,1:T(8,128)(2,1)S(1)} all-gather(bf16[48,1,256]{2,0,1:T(8,128)(2,1)} %param.13), channel_id=1, replica_groups=mesh['frame'=32,'tensor'=16] {'frame'}, dimensions={0}, use_global_device_ids=true | all-gather | bytes 811008 | tf_op jit(solution)/shard_map/all_gather | solution.py:51
  197.1 1.2 copy.16
  198.3 1.3 fusion.9
  199.5 0.0 all-to-all-done
  199.5 2.7 reshape.111
  202.3 0.0 all-gather.2.cloned.1.call-done
  202.3 0.0 copy-start.1
  202.3 4.2 %fusion.17 = bf16[512,256]{0,1:T(8,128)(2,1)S(1)} fusion(bf16[4096,256]{1,0:T(8,128)(2,1)} %param.10, bf16[512,1,4096]{2,0,1:T(8,128)(2,1)} %all-gather.2.cloned.1.call-done), kind=kOutput, calls=%fused_computation.16 | convolution fusion | flops 1074003968 | bytes 6553600 | tf_op jit(solution)/shard_map/dot_general | solution.py:37
  206.5 0.0 copy-done.1
  206.5 0.0 copy-start.2
  206.5 1.5 fusion
  208.0 2.0 fusion.2
  210.1 0.0 copy-done.2
  210.1 1.9 fusion.23
  212.0 0.0 copy-done
  212.0 3.2 fusion.1
  215.2 0.0 reduce-scatter.2.cloned.1.call-update
  215.2 144.6 %reduce-scatter.2.cloned.1.call-done = bf16[32,1,4096]{2,0,1:T(8,128)(2,1)} async-done(((bf16[512,1,4096]{2,0,1:T(8,128)(2,1)}), bf16[32,1,4096]{2,0,1:T(8,128)(2,1)}) %reduce-scatter.2.cloned.1.call-update) | async-done | bytes 262160 | tf_op jit(solution)/shard_map/reduce_scatter | solution.py:79
  (3 shorter events, 0.0 us)
Async XLA Ops:
  6.5 205.5 %copy-start = (bf16[256,4096]{1,0:T(8,128)(2,1)S(1)}, bf16[256,4096]{1,0:T(8,128)(2,1)}, u32[]{:S(2)}) copy-start(bf16[256,4096]{1,0:T(8,128)(2,1)} %param.11) | copy-start | bytes 6291460
  6.5 195.7 %all-gather.2.cloned.1.call-start = ((), (), s32[]{:S(2)}) async-start(), calls=%async_computation.2 | async-start | bytes 4456448 | tf_op jit(solution)/shard_map/all_gather | solution.py:38
  11.3 188.2 %all-to-all-start = ((bf16[32,48,1,256]{3,1,2,0:T(8,128)(2,1)}), bf16[32,48,1,256]{3,1,2,0:T(8,128)(2,1)}, u32[]{:S(2)}, u32[]{:S(2)}) async-start(bf16[32,48,1,256]{3,1,2,0:T(8,128)(2,1)} %stack.2), calls=%async_computation | async-start | bytes 1572864 | tf_op jit(solution)/shard_map/all_to_all | solution.py:13
  32.2 327.7 %reduce-scatter.2.cloned.1.call-start = ((), (), s32[]{:S(2)}) async-start(), calls=%async_computation.3 | async-start | bytes 4456448 | tf_op jit(solution)/shard_map/reduce_scatter | solution.py:79
  202.3 4.2 %copy-start.1 = (bf16[1536,2,128]{2,1,0:T(2,128)(2,1)S(1)}, bf16[1536,2,128]{2,1,0:T(2,128)(2,1)}, u32[]{:S(2)}) copy-start(bf16[1536,2,128]{2,1,0:T(2,128)(2,1)} %reshape.111) | copy-start | bytes 2359300
  206.5 3.6 copy-start.2
Sparse Core Ops, SparseCore 0:
  9.7 131.6 all-gather.1
  215.4 144.4 reduce-scatter.1

commit v2 on v0

--- a/solution.py
+++ b/solution.py
@@ -17,6 +17,16 @@
 def per_device(
     tokens, norm_gain, query_weight, out_weight, cache_keys, cache_values, token_pos, frame_pad
 ):
+
+    def state_the_pages(in_array, frame, peer_axis):
+        return jnp.split(
+            lax.all_gather(
+                jnp.concatenate([in_array, frame], axis=1), axis_name=peer_axis, axis=0, tiled=True
+            ),
+            [in_array.shape[1]],
+            axis=1,
+        )
+
     head_cols = query_weight.shape[1]
     heads_here = head_cols // HEAD_DIM
     seq_count = tokens.shape[1]
@@ -36,8 +46,7 @@
     valid_frames = all_frames - frame_pad
     start_max = jnp.full((query_rows, seq_count, heads_here), masked_score, jnp.float32)
     running_max = start_max
-    key_piece = lax.all_gather(cache_keys, "frame", axis=0, tiled=True)
-    value_piece = lax.all_gather(cache_values, "frame", axis=0, tiled=True)
+    key_piece, value_piece = state_the_pages(cache_keys, cache_values, "frame")
     row_count = key_piece.shape[0]
     frame_index = jnp.arange(row_count, dtype=jnp.int32)
     visible = (frame_index[None, None, :] <= token_pos[:, :, None]) & (

time: 465 us -> 367 us (0.79)
  the two profiles are of different devices: /device:TPU:12 before, /device:TPU:8 now
where the time goes in v2:
time: 367 us
  waiting for transfers between devices  320 us (87%)
  local copies, waits for them, and re-layouts  15.8 us (4%)
  between operations  13.8 us (4%)
  matrix products  10.8 us (3%)
  other arithmetic  6.58 us (2%)
    all_gather x1, waiting for transfers between devices, state_the_pages(): lax.all_gather(jnp.concatenate([in_array, frame], axis=1), axis_name=peer...  123 us
    reduce_scatter x1, waiting for transfers between devices, per_device(): lax.psum_scatter(jnp.dot(attended, out_weight, preferred_element_type=jnp...  113 us
    all_gather x1, waiting for transfers between devices, per_device(): lax.all_gather(outgoing, 'tensor', axis=0, tiled=True)  83.8 us
    split x2, local copies, waits for them, and re-layouts, state_the_pages(): jnp.split(lax.all_gather(jnp.concatenate([in_array, frame], axis=1), axis...  10.5 us
  transfers between devices with their start and end apart: 3, of which 3 were waited for; matrix products, arithmetic and copies ran while one was open for 5% of the time, Pallas kernels for 0%

profile of v2, /device:TPU:8, one launch (start us, length us, event | category | flops | bytes accessed | tf_op | source)
XLA Modules:
  0.0 366.8 jit_solution(1972710451527598370)
XLA Ops:
  6.5 0.0 copy-start
  6.5 0.0 all-gather.3.cloned.1.call-start
  6.5 0.9 pad_maximum_fusion
  7.4 0.7 copy.17
  8.1 0.0 all-gather.3.cloned.1.call-update
  8.1 0.0 all-gather.5.cloned.1.call-start
  8.2 1.1 fusion.26
  9.3 1.8 fusion.28
  11.1 0.0 all-gather.5.cloned.1.call-update
  11.1 0.0 reduce-scatter.2.cloned.1.call-start
  11.8 1.3 fusion.9
  13.1 123.0 %all-gather.3.cloned.1.call-done = bf16[1536,2,256]{2,1,0:T(2,128)(2,1)} async-done(((bf16[48,2,256]{2,1,0:T(2,128)(2,1)}), bf16[1536,2,256]{2,1,0:T(2,128)(2,1)}) %all-gather.3.cloned.1.call-update) | async-done | bytes 1572880 | tf_op jit(solution)/shard_map/all_gather | solution.py:23
  136.1 5.8 %fusion.31 = (bf16[1536,1,256]{2,1,0:T(2,128)(2,1)}, bf16[1536,1,256]{2,1,0:T(2,128)(2,1)}) fusion(bf16[1536,2,256]{2,1,0:T(2,128)(2,1)} %all-gather.3.cloned.1.call-done), kind=kLoop, calls=%fused_computation.30 | loop fusion | bytes 3145728 | tf_op jit(solution)/shard_map/split | solution.py:22
  141.9 4.7 %copy.26 = bf16[1536,1,256]{0,2,1:T(8,128)(2,1)} copy(bf16[1536,1,256]{2,1,0:T(2,128)(2,1)} %get-tuple-element.5) | data formatting | bytes 1572864
  146.6 4.7 %copy.18 = bf16[1536,1,256]{0,2,1:T(8,128)(2,1)} copy(bf16[1536,1,256]{2,1,0:T(2,128)(2,1)} %get-tuple-element.6) | data formatting | bytes 1572864 | tf_op jit(solution)/shard_map/split | solution.py:22
  151.3 83.8 %all-gather.5.cloned.1.call-done = bf16[512,1,4096]{2,0,1:T(8,128)(2,1)} async-done(((bf16[32,1,4096]{2,0,1:T(8,128)(2,1)}), bf16[512,1,4096]{2,0,1:T(8,128)(2,1)}) %all-gather.5.cloned.1.call-update) | async-done | bytes 4194320 | tf_op jit(solution)/shard_map/all_gather | solution.py:37
  235.0 0.0 copy-start.1
  235.0 4.2 %fusion.17 = bf16[512,256]{0,1:T(8,128)(2,1)S(1)} fusion(bf16[4096,256]{1,0:T(8,128)(2,1)} %param.10, bf16[512,1,4096]{2,0,1:T(8,128)(2,1)} %all-gather.5.cloned.1.call-done), kind=kOutput, calls=%fused_computation.16 | convolution fusion | flops 1074003968 | bytes 6553600 | tf_op jit(solution)/shard_map/dot_general | solution.py:36
  239.2 0.0 copy-done.1
  239.3 1.4 fusion
  240.6 0.0 copy-start.2
  240.6 1.5 fusion.2
  242.1 0.0 copy-done.2
  242.1 2.0 fusion.23
  244.2 0.0 copy-done
  244.2 3.2 fusion.1
  247.4 0.0 reduce-scatter.2.cloned.1.call-update
  247.4 112.9 %reduce-scatter.2.cloned.1.call-done = bf16[32,1,4096]{2,0,1:T(8,128)(2,1)} async-done(((bf16[512,1,4096]{2,0,1:T(8,128)(2,1)}), bf16[32,1,4096]{2,0,1:T(8,128)(2,1)}) %reduce-scatter.2.cloned.1.call-update) | async-done | bytes 262160 | tf_op jit(solution)/shard_map/reduce_scatter | solution.py:77
  (3 shorter events, 0.0 us)
Async XLA Ops:
  6.5 237.6 %copy-start = (bf16[256,4096]{1,0:T(8,128)(2,1)S(1)}, bf16[256,4096]{1,0:T(8,128)(2,1)}, u32[]{:S(2)}) copy-start(bf16[256,4096]{1,0:T(8,128)(2,1)} %param.11) | copy-start | bytes 6291460
  6.5 129.5 %all-gather.3.cloned.1.call-start = ((), (), s32[]{:S(2)}) async-start(), calls=%async_computation.1 | async-start | bytes 1622016 | tf_op jit(solution)/shard_map/all_gather | solution.py:23
  8.1 226.9 %all-gather.5.cloned.1.call-start = ((), (), s32[]{:S(2)}) async-start(), calls=%async_computation.2 | async-start | bytes 4456448 | tf_op jit(solution)/shard_map/all_gather | solution.py:37
  11.1 349.1 %reduce-scatter.2.cloned.1.call-start = ((), (), s32[]{:S(2)}) async-start(), calls=%async_computation.3 | async-start | bytes 4456448 | tf_op jit(solution)/shard_map/reduce_scatter | solution.py:77
  235.0 4.2 %copy-start.1 = (bf16[1536,1,256]{0,2,1:T(8,128)(2,1)S(1)}, bf16[1536,1,256]{0,2,1:T(8,128)(2,1)}, u32[]{:S(2)}) copy-start(bf16[1536,1,256]{0,2,1:T(8,128)(2,1)} %copy.26) | copy-start | bytes 2359300
  240.6 1.5 copy-start.2
Sparse Core Ops, SparseCore 0:
  11.7 124.3 all-gather.2
  138.2 96.8 all-gather.4
  247.5 112.6 reduce-scatter.1
